TPU v7x, 32 devices: a whole 2x2x4 slice. The times are simulated.
32 devices in a mesh: ctx: 2 (over y), exp: 16 (over z, x, core).
Axes of the slice: x: 2, y: 2, z: 4, core: 2. Of those that a mesh axis runs over, the one named last changes fastest.
Arguments:
- queries: bfloat16 [256, 8192], P('ctx', 'exp'), may hold values from -6 to 6
- keys: bfloat16 [256, 512], P('ctx'), may hold values from -6 to 6
- values: bfloat16 [256, 512], P('ctx'), may hold values from -5 to 5
- residual: bfloat16 [256, 4096], P(('ctx', 'exp')), may hold values from -6 to 6
- out_weight: bfloat16 [8192, 4096], P('exp'), may hold values from -0.125 to 0.125
- norm_gain: float32 [4096], replicated, may hold values from 0.25 to 1.75
- expert_ids: int32 [256, 8], P(('ctx', 'exp')), may hold values from 0 to 15, all different within a row; in each aligned block of 8 rows (0 to 7, 8 to 15, ...) at most 8 rows name the same one
- expert_gates: float32 [256, 8], P(('ctx', 'exp')), may hold values from 0.05 to 0.35
- w_gate: bfloat16 [16, 4096, 1536], P('exp', None, 'ctx'), may hold values from -0.09375 to 0.09375
- w_up: bfloat16 [16, 4096, 1536], P('exp', None, 'ctx'), may hold values from -0.09375 to 0.09375
- w_down: bfloat16 [16, 1536, 4096], P('exp', None, 'ctx'), may hold values from -0.3125 to 0.3125
Outputs:
- mixed: bfloat16 [256, 4096], P(('ctx', 'exp'))
- experts_out: bfloat16 [256, 4096], P(('ctx', 'exp'))
Inputs may be any that keep to these rules, and one draw needn't show every extreme that they name: `expert_ids`: in each aligned block of 8 rows (the rows of one device) no expert is named by more than 8 rows, a bound that some block reaches.
All inputs are finite; a program needn't handle non-finite values.
Results may differ from a plain program's by a relative error of at most 0.034.
Values may be sent and summed in bfloat16 or wider, within the bound.
A program may use at most 64 MiB of HBM per device.

v0:
```python
import jax
import jax.numpy as jnp
from jax import lax
from jax.sharding import PartitionSpec as P

QUERY_HEAD_COUNT = 64
KEY_VALUE_HEADS = 4
HEAD_WIDTH = 128


neg_large = -1e30
eps_norm = 1e-06


def shifted(value, axis, by):
    size = lax.axis_size(axis)
    pairs = [(i, i + by) for i in range(size) if 0 <= i + by < size]
    return lax.ppermute(value, axis, pairs)


def slot_numbers(expert_ids):
    tok_rows, top_count = expert_ids.shape
    flat_ids = expert_ids.reshape(-1)
    owner_row = jnp.arange(tok_rows * top_count, dtype=jnp.int32) // top_count
    earlier = (flat_ids[:, None] == flat_ids[None, :]) & (owner_row[None, :] < owner_row[:, None])
    return jnp.sum(earlier.astype(jnp.int32), axis=1).reshape(tok_rows, top_count)


def route_hits(expert_ids, slot_ids, expert_count, capacity):
    expert_hit = (
        expert_ids[None, None, :, :]
        == jnp.arange(expert_count, dtype=jnp.int32)[:, None, None, None]
    )
    slot_hit = (
        slot_ids[None, None, :, :] == jnp.arange(capacity, dtype=jnp.int32)[None, :, None, None]
    )
    return expert_hit & slot_hit


def expert_hidden(rows_block, gate_local, up_local):
    gate = jnp.dot(rows_block, gate_local, preferred_element_type=jnp.float32)
    upper = jnp.dot(rows_block, up_local, preferred_element_type=jnp.float32)
    return (jax.nn.silu(gate) * upper).astype(jnp.bfloat16)


def on_device(
    queries,
    keys,
    values,
    residual,
    out_weight,
    norm_gain,
    expert_ids,
    expert_gates,
    w_gate,
    w_up,
    w_down,
):
    tok_query = queries.shape[0]
    device_share = queries.shape[1] // HEAD_WIDTH
    ctx_pos = lax.axis_index("ctx")
    key_value_head = lax.axis_index("exp") * device_share // (QUERY_HEAD_COUNT // KEY_VALUE_HEADS)
    own_keys = lax.dynamic_slice_in_dim(keys, key_value_head * HEAD_WIDTH, HEAD_WIDTH, 1)
    own_values = lax.dynamic_slice_in_dim(values, key_value_head * HEAD_WIDTH, HEAD_WIDTH, 1)
    own_block = jnp.stack([own_keys, own_values])
    query_heads = queries.reshape(tok_query, device_share, HEAD_WIDTH)
    query_start = ctx_pos * tok_query
    query_pos = query_start + jnp.arange(tok_query, dtype=jnp.int32)
    scale = 1.0 / HEAD_WIDTH**0.5
    start_state = (
        jnp.full((device_share, tok_query), neg_large, jnp.float32),
        jnp.zeros((device_share, tok_query), jnp.float32),
        jnp.zeros((device_share, tok_query, HEAD_WIDTH), jnp.float32),
    )

    def attend(state_now, kv_piece, key_start):

        def compute(current):
            running_max, running_sum, weighted = current
            key_pos = key_start + jnp.arange(kv_piece.shape[1], dtype=jnp.int32)
            allowed = key_pos[None, :] <= query_pos[:, None]
            scores = (
                jnp.einsum(
                    "qhd,kd->hqk", query_heads, kv_piece[0], preferred_element_type=jnp.float32
                )
                * scale
            )
            scores = jnp.where(allowed[None], scores, neg_large)
            new_max = jnp.maximum(running_max, jnp.max(scores, axis=2))
            weights_blk = jnp.where(allowed[None], jnp.exp(scores - new_max[:, :, None]), 0.0)
            shrink = jnp.exp(running_max - new_max)
            new_sum = running_sum * shrink + jnp.sum(weights_blk, axis=2)
            added = jnp.einsum(
                "hqk,kd->hqd",
                weights_blk.astype(jnp.bfloat16),
                kv_piece[1],
                preferred_element_type=jnp.float32,
            )
            return (new_max, new_sum, weighted * shrink[:, :, None] + added)

        def unchanged(current):
            return current

        useful = (key_start >= 0) & (key_start <= query_start + tok_query - 1)
        return lax.cond(useful, compute, unchanged, state_now)

    ctx_count = lax.axis_size("ctx")
    state_now = attend(start_state, own_block, query_start)

    def cycle_turn(cycle_step, carried):
        state_cur, moving = carried
        moving = shifted(moving, "ctx", 1)
        source = ctx_pos - cycle_step
        return (attend(state_cur, moving, source * tok_query), moving)

    state_now, _ = lax.fori_loop(1, ctx_count, cycle_turn, (state_now, own_block))
    running_max, running_sum, weighted = state_now
    heads_done = (weighted / running_sum[:, :, None]).astype(jnp.bfloat16)
    heads_done = jnp.transpose(heads_done, (1, 0, 2)).reshape(tok_query, device_share * HEAD_WIDTH)
    tok_rows, top_count = expert_ids.shape
    projected = lax.psum_scatter(
        jnp.dot(heads_done, out_weight, preferred_element_type=jnp.float32).astype(jnp.bfloat16),
        "exp",
        scatter_dimension=0,
        tiled=True,
    ).astype(jnp.float32)
    mixed = (residual.astype(jnp.float32) + projected).astype(jnp.bfloat16)
    stream = mixed.astype(jnp.float32)
    mean_sq = jnp.mean(stream * stream, axis=1, keepdims=True)
    normed = (stream * lax.rsqrt(mean_sq + eps_norm) * norm_gain[None, :]).astype(jnp.bfloat16)
    expert_count = lax.axis_size("exp")
    ctx_count = lax.axis_size("ctx")
    capacity = min(tok_rows, 2 * tok_rows * top_count // expert_count)
    slot_ids = slot_numbers(expert_ids)
    hits = route_hits(expert_ids, slot_ids, expert_count, capacity)
    send_table = jnp.any(hits, axis=3).astype(jnp.bfloat16)
    gate_local = w_gate[0]
    up_local = w_up[0]
    down_local = w_down[0]
    width = normed.shape[1]
    outgoing = jnp.einsum(
        "ecm,md->ecd", send_table, normed, preferred_element_type=jnp.float32
    ).astype(jnp.bfloat16)
    arrived = lax.all_to_all(outgoing, "exp", split_axis=0, concat_axis=0, tiled=True)
    local_rows = arrived.reshape(-1, width)
    hidden = expert_hidden(
        lax.all_gather(local_rows, "ctx", axis=0, tiled=True), gate_local, up_local
    )
    expert_result = jnp.dot(
        lax.all_gather(hidden, "ctx", axis=1, tiled=True),
        down_local,
        preferred_element_type=jnp.float32,
    ).astype(jnp.bfloat16)
    expert_result = expert_result.reshape(ctx_count, expert_count, capacity, down_local.shape[1])
    returned = lax.all_to_all(
        lax.all_to_all(expert_result, "ctx", split_axis=0, concat_axis=3, tiled=True),
        "exp",
        split_axis=1,
        concat_axis=0,
        tiled=True,
    )
    returned = returned.reshape(expert_count, capacity, width)
    mix_table = jnp.sum(jnp.where(hits, expert_gates[None, None, :, :], 0.0), axis=3)
    experts_out = jnp.einsum(
        "ecm,ecd->md", mix_table, returned.astype(jnp.float32), precision=lax.Precision.HIGHEST
    )
    return (mixed, experts_out.astype(jnp.bfloat16))


def solution(mesh):
    return jax.shard_map(
        on_device,
        mesh=mesh,
        in_specs=(
            P("ctx", "exp"),
            P("ctx", None),
            P("ctx", None),
            P(("ctx", "exp"), None),
            P("exp", None),
            P(),
            P(("ctx", "exp"), None),
            P(("ctx", "exp"), None),
            P("exp", None, "ctx"),
            P("exp", None, "ctx"),
            P("exp", None, "ctx"),
        ),
        out_specs=(P(("ctx", "exp"), None), P(("ctx", "exp"), None)),
        check_vma=False,
    )
```

profile of v0, /device:TPU:1, one launch (start us, length us, event | category | flops | bytes accessed | tf_op | source)
XLA Modules:
  0.0 221.7 jit_solution(4752855502941441727)
XLA Ops:
  7.2 0.0 reduce-scatter.2.cloned.1.call-start
  7.2 0.8 constant_dynamic-slice_fusion
  8.0 4.0 %collective-permute-start = (bf16[2,128,128]{2,1,0:T(8,128)(2,1)S(1)}, bf16[2,128,128]{2,1,0:T(8,128)(2,1)S(1)}, u32[]{:S(2)}, u32[]{:S(2)}) collective-permute-start(bf16[2,128,128]{2,1,0:T(8,128)(2,1)S(1)} %pad_maximum_fusion), channel_id=1, source_target_pairs={{0,16},{1,17},{2,18},{3,19},{4,20},{5,21},{6,22},{7,23},{8,24},{9,... | collective-permute-start | bytes 196616 | tf_op jit(solution)/shard_map/while/body/eval_jaxpr/ppermute | solution.py:18
  12.0 1.0 copy.33
  13.1 3.3 %conditional.2 = (f32[4,128]{1,0:T(4,128)}, f32[4,128]{1,0:T(4,128)S(1)}, f32[4,128,128]{2,1,0:T(8,128)S(1)}) conditional(s32[]{:T(128)} %convert_element_type.54, () %tuple.30, (s32[]{:T(128)}, s32[128]{0:T(128)S(1)}, bf16[128,128]{1,0:T(8,128)(2,1)S(1)}, bf16[128,4,128]{0,2,1:T(8,128)(2,1)S(1)}, bf16[128,128]{1,0:T(8,128)(2,1)S(1)}) %tuple.57), branch_computations={%region_0.1_spmd, %region_1.4_spmd} | conditional | flops 34228352 | bytes 1334812 | solution.py:105
  13.1 0.1 broadcast_compare_fusion
  13.2 0.2 fusion.51
  13.4 0.6 exponential_multiply_fusion
  14.0 0.7 fusion.3
  14.7 0.7 fusion.11
  15.4 0.9 convolution_add_fusion
  16.3 0.0 collective-permute-done
  16.3 0.0 copy-start.3
  16.4 0.0 copy-start.1
  16.4 0.2 conditional.3
  16.4 0.1 copy.44
  16.5 0.0 copy-start.2
  16.6 3.9 %convolution_convert_fusion.1 = bf16[128,4096]{1,0:T(8,128)(2,1)} fusion(bf16[128,512]{0,1:T(8,128)(2,1)S(1)} %bitcast.77, bf16[512,4096]{1,0:T(8,128)(2,1)} %param.19), kind=kOutput, calls=%fused_computation.44 | convolution fusion | flops 537395200 | bytes 5373952 | tf_op jit(solution)/shard_map/dot_general | solution.py:122
  20.5 0.0 reduce-scatter.2.cloned.1.call-update
  20.5 0.0 all-gather.2.cloned.1.call-start
  20.6 0.0 copy-done.3
  20.6 0.1 eq.56
  20.7 0.2 convert_reduce_fusion
  20.8 0.1 eq.60
  20.9 0.1 iota_compare_fusion.1
  21.0 0.2 and_reduce_fusion
  21.2 0.1 copy.37
  21.3 56.8 %reduce-scatter.2.cloned.1.call-done = bf16[8,4096]{1,0:T(8,128)(2,1)} async-done(((bf16[128,4096]{1,0:T(8,128)(2,1)}), bf16[8,4096]{1,0:T(8,128)(2,1)}) %reduce-scatter.2.cloned.1.call-update) | async-done | bytes 65552 | tf_op jit(solution)/shard_map/reduce_scatter | solution.py:121
  78.1 0.0 copy-done.1
  78.1 1.0 fusion.44
  79.1 0.0 copy-start
  79.1 0.0 copy-done.2
  79.1 0.5 convolution_convert_fusion
  79.6 31.3 %all_to_all.32 = bf16[16,8,4096]{2,1,0:T(8,128)(2,1)} all-to-all(bf16[16,8,4096]{2,1,0:T(8,128)(2,1)S(1)} %convolution_convert_fusion), channel_id=1, replica_groups=mesh['ctx'=2,'exp'=16] {'exp'}, dimensions={0} | all-to-all | bytes 2097152 | tf_op jit(solution)/shard_map/all_to_all | solution.py:144
  110.9 0.0 all-gather.2.cloned.1.call-update
  110.9 32.6 %all-gather.2.cloned.1.call-done = bf16[256,4096]{1,0:T(8,128)(2,1)} async-done(((bf16[128,4096]{1,0:T(8,128)(2,1)}), bf16[256,4096]{1,0:T(8,128)(2,1)}) %all-gather.2.cloned.1.call-update) | async-done | bytes 2097168 | tf_op jit(solution)/shard_map/all_gather | solution.py:147
  143.5 0.0 copy-start.5
  143.5 0.0 slice-start
  143.5 5.3 %fusion.29 = f32[256,768]{1,0:T(8,128)S(1)} fusion(bf16[256,4096]{1,0:T(8,128)(2,1)} %all-gather.2.cloned.1.call-done, bf16[1,4096,768]{2,1,0:T(8,128)(2,1)} %param.23), kind=kOutput, calls=%fused_computation.41 | convolution fusion | flops 1610612736 | bytes 9175040 | tf_op jit(solution)/shard_map/dot_general | solution.py:41
  148.9 0.0 copy-done
  148.9 0.0 copy-done.5
  148.9 0.0 slice-start.1
  148.9 4.8 %fusion.38 = bf16[256,768]{1,0:T(8,128)(2,1)S(1)} fusion(bf16[256,4096]{1,0:T(8,128)(2,1)S(1)} %copy-done.5, bf16[1,4096,768]{2,1,0:T(8,128)(2,1)} %param.24, f32[256,768]{1,0:T(8,128)S(1)} %fusion.29), kind=kOutput, calls=%fused_computation.49 | convolution fusion | flops 1611792384 | bytes 9568256 | tf_op jit(solution)/shard_map/dot_general | solution.py:42
  153.7 10.7 %all_gather.7 = bf16[256,1536]{1,0:T(8,128)(2,1)S(1)} all-gather(bf16[256,768]{1,0:T(8,128)(2,1)S(1)} %fusion.38), channel_id=1, replica_groups=mesh['ctx'=2,'exp'=16] {'ctx'}, dimensions={1}, use_global_device_ids=true | all-gather | bytes 1179648 | tf_op jit(solution)/shard_map/all_gather | solution.py:150
  164.4 0.0 slice-done
  164.4 0.0 slice-done.1
  164.4 1.8 fusion.32
  166.2 0.0 copy-start.4
  166.2 14.5 %all_to_all.33 = bf16[2,16,8,2048]{3,2,1,0:T(8,128)(2,1)S(1)} all-to-all(bf16[2,16,8,2048]{3,2,1,0:T(8,128)(2,1)S(1)} %bitcast.76), channel_id=1, replica_groups=mesh['ctx'=2,'exp'=16] {'ctx'}, dimensions={0} | all-to-all | bytes 2097152 | tf_op jit(solution)/shard_map/all_to_all | solution.py:156
  180.7 1.0 copy.38
  181.7 8.0 %all-to-all-start.2 = ((bf16[1,16,8,4096]{3,2,0,1:T(8,128)(2,1)}), bf16[1,16,8,4096]{3,2,0,1:T(8,128)(2,1)S(1)}, u32[]{:S(2)}, u32[]{:S(2)}) async-start(bf16[1,16,8,4096]{3,2,0,1:T(8,128)(2,1)} %bitcast.21), calls=%async_computation.3 | async-start | bytes 2097152 | tf_op jit(solution)/shard_map/all_to_all | solution.py:155
  189.7 0.0 copy-done.4
  189.7 0.2 fusion.43
  189.9 22.9 %all-to-all-done.2 = bf16[1,16,8,4096]{3,2,0,1:T(8,128)(2,1)S(1)} async-done(((bf16[1,16,8,4096]{3,2,0,1:T(8,128)(2,1)}), bf16[1,16,8,4096]{3,2,0,1:T(8,128)(2,1)S(1)}, u32[]{:S(2)}, u32[]{:S(2)}) %all-to-all-start.2) | async-done | bytes 1048608 | tf_op jit(solution)/shard_map/all_to_all | solution.py:155
  212.9 2.0 fusion.31
  (8 shorter events, 0.1 us)
Async XLA Ops:
  7.2 70.9 %reduce-scatter.2.cloned.1.call-start = ((), (), s32[]{:S(2)}) async-start(), calls=%async_computation.4 | async-start | bytes 1114112 | tf_op jit(solution)/shard_map/reduce_scatter | solution.py:121
  8.0 8.3 %collective-permute-start = (bf16[2,128,128]{2,1,0:T(8,128)(2,1)S(1)}, bf16[2,128,128]{2,1,0:T(8,128)(2,1)S(1)}, u32[]{:S(2)}, u32[]{:S(2)}) collective-permute-start(bf16[2,128,128]{2,1,0:T(8,128)(2,1)S(1)} %pad_maximum_fusion), channel_id=1, source_target_pairs={{0,16},{1,17},{2,18},{3,19},{4,20},{5,21},{6,22},{7,23},{8,24},{9,... | collective-permute-start | bytes 196616 | tf_op jit(solution)/shard_map/while/body/eval_jaxpr/ppermute | solution.py:18
  16.3 4.2 %copy-start.3 = (s32[8,8]{1,0:T(8,128)S(1)}, s32[8,8]{1,0:T(8,128)}, u32[]{:S(2)}) copy-start(s32[8,8]{1,0:T(8,128)} %param.21) | copy-start | bytes 772
  16.4 61.8 %copy-start.1 = (bf16[8,4096]{1,0:T(8,128)(2,1)S(1)}, bf16[8,4096]{1,0:T(8,128)(2,1)}, u32[]{:S(2)}) copy-start(bf16[8,4096]{1,0:T(8,128)(2,1)} %param.18) | copy-start | bytes 196612
  16.5 62.6 %copy-start.2 = (f32[4096]{0:T(1024)S(1)}, f32[4096]{0:T(1024)}, u32[]{:S(2)}) copy-start(f32[4096]{0:T(1024)} %param.20) | copy-start | bytes 49156
  20.5 123.0 %all-gather.2.cloned.1.call-start = ((), (), s32[]{:S(2)}) async-start(), calls=%async_computation.5 | async-start | bytes 3145728 | tf_op jit(solution)/shard_map/all_gather | solution.py:147
  79.1 69.8 %copy-start = (bf16[8,4096]{1,0:T(8,128)(2,1)}, bf16[8,4096]{1,0:T(8,128)(2,1)S(1)}, u32[]{:S(2)}) copy-start(bf16[8,4096]{1,0:T(8,128)(2,1)S(1)} %get-tuple-element.142) | copy-start | bytes 196612
  143.5 5.4 %copy-start.5 = (bf16[256,4096]{1,0:T(8,128)(2,1)S(1)}, bf16[256,4096]{1,0:T(8,128)(2,1)}, u32[]{:S(2)}) copy-start(bf16[256,4096]{1,0:T(8,128)(2,1)} %all-gather.2.cloned.1.call-done) | copy-start | bytes 6291460
  143.5 20.8 %slice-start = ((s8[6291456]{0:T(1024)(128)(4,1)}), s8[4194304]{0:T(1024)(128)(4,1)S(1)}, s32[]{:S(2)}) async-start(s8[6291456]{0:T(1024)(128)(4,1)} %bitcast.80), calls=%async_computation.6 | async-start | bytes 8388608
  148.9 15.5 %slice-start.1 = ((s8[6291456]{0:T(1024)(128)(4,1)}), s8[2097152]{0:T(1024)(128)(4,1)S(1)}, s32[]{:S(2)}) async-start(s8[6291456]{0:T(1024)(128)(4,1)} %bitcast.80), calls=%async_computation.7 | async-start | bytes 4194304
  166.2 23.6 %copy-start.4 = (f32[8,8]{1,0:T(8,128)S(1)}, f32[8,8]{1,0:T(8,128)}, u32[]{:S(2)}) copy-start(f32[8,8]{1,0:T(8,128)} %param.22) | copy-start | bytes 772
  181.7 31.1 %all-to-all-start.2 = ((bf16[1,16,8,4096]{3,2,0,1:T(8,128)(2,1)}), bf16[1,16,8,4096]{3,2,0,1:T(8,128)(2,1)S(1)}, u32[]{:S(2)}, u32[]{:S(2)}) async-start(bf16[1,16,8,4096]{3,2,0,1:T(8,128)(2,1)} %bitcast.21), calls=%async_computation.3 | async-start | bytes 2097152 | tf_op jit(solution)/shard_map/all_to_all | solution.py:155
Sparse Core Ops, SparseCore 0:
  20.6 57.4 reduce-scatter.1
  111.0 32.4 all-gather.1
where the time goes:
time: 223 us; the launch traced here: 222 us
  waiting for transfers between devices  112 us (50%)
  blocking collectives  56.5 us (25%)
  matrix products  19.4 us (9%)
  between operations  14.3 us (6%)
  starting transfers between devices  12 us (5%)
  other arithmetic  3.76 us (2%)
  local copies, waits for them, and re-layouts  3.28 us (1%)
    reduce_scatter x1, waiting for transfers between devices, on_device(): lax.psum_scatter(jnp.dot(heads_done, out_weight, preferred_element_type=j...  56.8 us
    all_gather x1, waiting for transfers between devices, on_device(): lax.all_gather(local_rows, 'ctx', axis=0, tiled=True)  32.6 us
    all_to_all x1, blocking collectives, on_device(): lax.all_to_all(outgoing, 'exp', split_axis=0, concat_axis=0, tiled=True)  31.3 us
    all_to_all x1, waiting for transfers between devices, on_device(): lax.all_to_all(lax.all_to_all(expert_result, 'ctx', split_axis=0, concat_...  22.9 us
    all_to_all x1, blocking collectives, on_device(): lax.all_to_all(expert_result, 'ctx', split_axis=0, concat_axis=3, tiled=T...  14.5 us
    all_gather x1, blocking collectives, on_device(): lax.all_gather(hidden, 'ctx', axis=1, tiled=True)  10.7 us
    all_to_all x1, starting transfers between devices, on_device(): lax.all_to_all(lax.all_to_all(expert_result, 'ctx', split_axis=0, concat_...  7.97 us
    dot_general x1, matrix products, expert_hidden(): gate = jnp.dot(rows_block, gate_local, preferred_element_type=jnp.float32)  5.35 us
  transfers between devices with their start and end apart: 4, of which 3 were waited for; matrix products, arithmetic and copies ran while one was open for 2% of the time, Pallas kernels for 0%

commit v1 on v0

--- a/solution.py
+++ b/solution.py
@@ -1,6 +1,8 @@
 import jax
 import jax.numpy as jnp
 from jax import lax
+from jax.experimental import pallas as pl
+from jax.experimental.pallas import tpu as pltpu
 from jax.sharding import PartitionSpec as P
 
 QUERY_HEAD_COUNT = 64
@@ -167,9 +169,423 @@
     return (mixed, experts_out.astype(jnp.bfloat16))
 
 
+BF = jnp.bfloat16
+F32 = jnp.float32
+ROWS = 16
+EXTRA = 128
+PROJ_PARTS = 4
+FF_PARTS = 3
+OUT_PARTS = 2
+
+
+def layer_kernel(
+    queries,
+    keys,
+    values,
+    residual,
+    norm_gain,
+    expert_ids,
+    expert_gates,
+    wo_hbm,
+    wg_hbm,
+    wu_hbm,
+    wd_hbm,
+    mixed_out,
+    experts_out,
+    wo,
+    wg,
+    wu,
+    wd,
+    kv,
+    res,
+    table,
+    heads,
+    pc_send,
+    pc_recv,
+    px_send,
+    px_recv,
+    pz_send,
+    pz_recv,
+    proj,
+    mixed_rows,
+    rows_all,
+    hidden,
+    oc_send,
+    oc_recv,
+    ox_send,
+    ox_recv,
+    oz_send,
+    oz_recv,
+    eo,
+    eo_recv,
+    w_sem,
+    send_sem,
+    recv_sem,
+):
+    y = lax.axis_index("ctx")
+    e = lax.axis_index("exp")
+    z, x, k = e // 4, (e // 2) % 2, e % 2
+    width = mixed_out.shape[1]
+    half = width // 2
+    cols = half // PROJ_PARTS
+    ff = hidden.shape[2]
+    ff_cols = ff // FF_PARTS
+    out_half = width // 4
+    out_cols = out_half // OUT_PARTS
+    tokens = queries.shape[0]
+
+    def device(yy, zz, xx, kk):
+        return (yy, zz * 4 + xx * 2 + kk)
+
+    other_core = device(y, z, x, 1 - k)
+    x_next = device(y, z, 1 - x, k)
+    y_next = device(1 - y, z, x, k)
+    partners = [other_core, x_next]
+    for dy in range(2):
+        for dz in range(4):
+            if dy or dz:
+                partners.append(device((y + dy) % 2, (z + dz) % 4, x, k))
+
+    weight_copies = {}
+
+    def fetch(name, src, dst):
+        copy = pltpu.make_async_copy(src, dst, w_sem.at[len(weight_copies)])
+        weight_copies[name] = copy
+        copy.start()
+
+    fetch("wo", wo_hbm, wo)
+
+    barrier = pltpu.get_barrier_semaphore()
+    for partner in partners:
+        pl.semaphore_signal(barrier, inc=1, device_id=partner, device_id_type=pl.DeviceIdType.MESH)
+
+    kvh = e * (queries.shape[1] // HEAD_WIDTH) // (QUERY_HEAD_COUNT // KEY_VALUE_HEADS)
+    kv_cols = pl.ds(pl.multiple_of(kvh * HEAD_WIDTH, HEAD_WIDTH), HEAD_WIDTH)
+    kv[y, 0] = keys[:, kv_cols]
+    kv[y, 1] = values[:, kv_cols]
+    res[k] = residual[...].astype(F32)
+    lanes = lax.broadcasted_iota(jnp.int32, (expert_ids.shape[0], EXTRA), 1) % 64
+    gate_rows = jnp.zeros(lanes.shape, F32)
+    for slot in range(expert_ids.shape[1]):
+        gate_rows += jnp.where(
+            expert_ids[:, slot : slot + 1] == lanes, expert_gates[:, slot : slot + 1], 0.0
+        )
+    table[k] = gate_rows
+
+    pl.semaphore_wait(barrier, len(partners))
+
+    sent = []
+
+    def send(src, dst, to):
+        number = len(sent)
+        copy = pltpu.make_async_remote_copy(
+            src_ref=src,
+            dst_ref=dst,
+            send_sem=send_sem.at[number],
+            recv_sem=recv_sem.at[number],
+            device_id=to,
+            device_id_type=pl.DeviceIdType.MESH,
+        )
+        copy.start()
+        sent.append(copy)
+        return copy
+
+    kv_copy = send(kv.at[y], kv.at[y], y_next)
+    res_copy = send(res.at[k], res.at[k], other_core)
+    table_copy = send(table.at[k], table.at[k], other_core)
+    fetch("wg", wg_hbm.at[0], wg)
+    fetch("wu", wu_hbm.at[0], wu)
+    fetch("wd", wd_hbm.at[0], wd)
+
+    kv_copy.wait_recv()
+    key_all = kv[:, 0].reshape(2 * tokens, HEAD_WIDTH)
+    value_all = kv[:, 1].reshape(2 * tokens, HEAD_WIDTH)
+    shape = (tokens, 2 * tokens)
+    allowed = lax.broadcasted_iota(jnp.int32, shape, 1) <= y * tokens + lax.broadcasted_iota(
+        jnp.int32, shape, 0
+    )
+    scale = 1.0 / HEAD_WIDTH**0.5
+    for head in range(queries.shape[1] // HEAD_WIDTH):
+        span = slice(head * HEAD_WIDTH, (head + 1) * HEAD_WIDTH)
+        scores = (
+            lax.dot_general(
+                queries[:, span], key_all, (((1,), (1,)), ((), ())), preferred_element_type=F32
+            )
+            * scale
+        )
+        scores = jnp.where(allowed, scores, neg_large)
+        weights = jnp.where(
+            allowed, jnp.exp(scores - jnp.max(scores, axis=1, keepdims=True)), 0.0
+        )
+        total = jnp.sum(weights, axis=1, keepdims=True)
+        numer = jnp.dot(weights.astype(BF), value_all, preferred_element_type=F32)
+        heads[:, span] = (numer / total).astype(BF)
+
+    def columns(which, part, span, size):
+        return pl.ds(pl.multiple_of(which * span + part * size, size), size)
+
+    weight_copies["wo"].wait()
+    to_core = []
+    for part in range(PROJ_PARTS):
+        piece = jnp.dot(
+            heads[...], wo[:, columns(1 - k, part, half, cols)], preferred_element_type=F32
+        )
+        pc_send[part] = piece.astype(BF)
+        to_core.append(send(pc_send.at[part], pc_recv.at[part], other_core))
+    to_x = []
+    for part in range(PROJ_PARTS):
+        piece = jnp.dot(
+            heads[...], wo[:, columns(k, part, half, cols)], preferred_element_type=F32
+        )
+        to_core[part].wait_recv()
+        piece = (piece + pc_recv[part].astype(F32)).astype(BF)
+        for chip in range(tokens // ROWS):
+            px_send[part, chip % 2, chip // 2] = piece[chip * ROWS : (chip + 1) * ROWS]
+        to_x.append(send(px_send.at[part, 1 - x], px_recv.at[part], x_next))
+    to_z = []
+    for part in range(PROJ_PARTS):
+        to_x[part].wait_recv()
+        pz_send[part] = (px_send[part, x].astype(F32) + px_recv[part].astype(F32)).astype(BF)
+        for dz in range(1, 4):
+            zz = (z + dz) % 4
+            to_z.append(
+                send(pz_send.at[part, zz], pz_recv.at[part, dz - 1], device(y, zz, x, k))
+            )
+    back = []
+    for part in range(PROJ_PARTS):
+        piece = pz_send[part, z].astype(F32)
+        for dz in range(1, 4):
+            to_z[part * 3 + dz - 1].wait_recv()
+            piece += pz_recv[part, dz - 1].astype(F32)
+        place = columns(k, part, half, cols)
+        proj[:, place] = piece
+        back.append(send(proj.at[:, place], proj.at[:, place], other_core))
+
+    res_copy.wait_recv()
+    table_copy.wait_recv()
+    for copy in back:
+        copy.wait_recv()
+    stream = (proj[...] + res[...].reshape(ROWS, width)).astype(BF).astype(F32)
+    mean_sq = jnp.mean(stream * stream, axis=1, keepdims=True)
+    normed = (stream * lax.rsqrt(mean_sq + eps_norm) * norm_gain[...]).astype(BF)
+    gates = table[...].reshape(ROWS, EXTRA)
+    gate_high = gates.astype(BF).astype(F32)
+    gate_lane = lax.broadcasted_iota(jnp.int32, gates.shape, 1)
+    gates = jnp.where(gate_lane < 64, gate_high, gates - gate_high).astype(BF)
+
+    def block(xx, yy, zz):
+        return (xx * 2 + yy) * 4 + zz
+
+    own = block(x, y, z)
+    for side in range(2):
+        rows_all[side, own, :, :half] = normed[:, side * half : (side + 1) * half]
+        rows_all[side, own, :, half:] = gates
+
+    def pass_on(number, to):
+        place = rows_all.at[k, number]
+        return send(place, place, to)
+
+    y1, x1 = y + k * (1 - 2 * y), x + (1 - k) * (1 - 2 * x)
+    y2, x2 = y + (1 - k) * (1 - 2 * y), x + k * (1 - 2 * x)
+    first_to, second_to = device(y1, z, x1, k), device(y2, z, x2, k)
+    along_z = [
+        pass_on(own, device(y, (z + dz) % 4, x, k)) for dz in range(1, 4)
+    ]
+    first, second, second_far, cross = [], [], [], []
+    first.append(pass_on(own, first_to))
+    second.append(pass_on(own, second_to))
+    mixed_rows[...] = stream.reshape(2, ROWS // 2, width)
+    mixed_out[...] = mixed_rows[k].astype(BF)
+    for i in range(1, 4):
+        along_z[i - 1].wait_recv()
+        number = block(x, y, (z + 4 - i) % 4)
+        first.append(pass_on(number, first_to))
+        second.append(pass_on(number, second_to))
+        cross.append(pass_on(number, other_core))
+    for i in range(4):
+        first[i].wait_recv()
+        number = block(x1, y1, (z + 4 - i) % 4)
+        second_far.append(pass_on(number, second_to))
+        cross.append(pass_on(number, other_core))
+    for i in range(4):
+        second[i].wait_recv()
+        cross.append(pass_on(block(x2, y2, (z + 4 - i) % 4), other_core))
+    for i in range(4):
+        second_far[i].wait_recv()
+        cross.append(pass_on(block(1 - x, 1 - y, (z + 4 - i) % 4), other_core))
+    weight_copies["wg"].wait()
+    weight_copies["wu"].wait()
+    for copy in cross:
+        copy.wait_recv()
+
+    all_tokens = rows_all.shape[1] * ROWS
+    across = []
+    for part in range(FF_PARTS):
+        span = slice(part * ff_cols, (part + 1) * ff_cols)
+        gate = jnp.zeros((all_tokens, ff_cols), F32)
+        upper = jnp.zeros((all_tokens, ff_cols), F32)
+        for side in range(2):
+            rows = rows_all[side, :, :, :half].reshape(all_tokens, half)
+            depth = slice(side * half, (side + 1) * half)
+            gate += jnp.dot(rows, wg[depth, span], preferred_element_type=F32)
+            upper += jnp.dot(rows, wu[depth, span], preferred_element_type=F32)
+        hidden[y, :, span] = (gate / (1.0 + jnp.exp(-gate)) * upper).astype(BF)
+        place = hidden.at[y, :, span]
+        across.append(send(place, place, y_next))
+    picked = rows_all[0, :, :, half:].reshape(all_tokens, EXTRA).astype(F32)
+    picked_lane = lax.broadcasted_iota(jnp.int32, picked.shape, 1) % 64
+    share = jnp.sum(jnp.where(picked_lane == e, picked, 0.0), axis=1, keepdims=True)
+    weight_copies["wd"].wait()
+    for copy in across:
+        copy.wait_recv()
+
+    def down(which, part):
+        place = columns(which, part, out_half, out_cols)
+        result = jnp.dot(hidden[0], wd[:ff, place], preferred_element_type=F32)
+        result += jnp.dot(hidden[1], wd[ff:, place], preferred_element_type=F32)
+        return result * share
+
+    to_core, to_x, to_z = [], [], []
+    for part in range(OUT_PARTS):
+        oc_send[part] = down(1 - k, part).astype(BF)
+        to_core.append(send(oc_send.at[part], oc_recv.at[part], other_core))
+    for part in range(OUT_PARTS):
+        piece = down(k, part)
+        to_core[part].wait_recv()
+        piece = (piece + oc_recv[part].astype(F32)).astype(BF)
+        ox_send[part] = piece.reshape(2, 8, ROWS, out_cols)
+        to_x.append(send(ox_send.at[part, 1 - x], ox_recv.at[part], x_next))
+    for part in range(OUT_PARTS):
+        to_x[part].wait_recv()
+        oz_send[part] = (ox_send[part, x].astype(F32) + ox_recv[part].astype(F32)).astype(BF)
+        for dy in range(2):
+            for dz in range(4):
+                if dy or dz:
+                    yy, zz = (y + dy) % 2, (z + dz) % 4
+                    to_z.append(
+                        send(
+                            oz_send.at[part, yy * 4 + zz],
+                            oz_recv.at[part, dy * 4 + dz],
+                            device(yy, zz, x, k),
+                        )
+                    )
+                else:
+                    to_z.append(None)
+    back = []
+    for part in range(OUT_PARTS):
+        for dy in range(2):
+            piece = None
+            for dz in range(4):
+                copy = to_z[part * 8 + dy * 4 + dz]
+                if copy is None:
+                    piece = oz_send[part, y * 4 + z].astype(F32)
+                    continue
+                copy.wait_recv()
+                came = oz_recv[part, dy * 4 + dz].astype(F32)
+                piece = came if piece is None else piece + came
+            side = y + dy * (1 - 2 * y)
+            place = columns(side * 2 + k, part, out_half, out_cols)
+            eo[:, :, place] = piece.reshape(2, ROWS // 2, out_cols)
+            back.append(send(eo.at[1 - k, :, place], eo_recv.at[:, place], other_core))
+    for part in range(OUT_PARTS):
+        for side in range(2):
+            place = columns(side * 2 + k, part, out_half, out_cols)
+            experts_out[:, place] = eo[k, :, place].astype(BF)
+    for copy in back:
+        copy.wait_recv()
+    for part in range(OUT_PARTS):
+        for side in range(2):
+            place = columns(side * 2 + 1 - k, part, out_half, out_cols)
+            experts_out[:, place] = eo_recv[:, place].astype(BF)
+    for copy in sent:
+        copy.wait_send()
+
+
+def layer_on_device(
+    queries,
+    keys,
+    values,
+    residual,
+    out_weight,
+    norm_gain,
+    expert_ids,
+    expert_gates,
+    w_gate,
+    w_up,
+    w_down,
+):
+    tokens, head_cols = queries.shape
+    own_rows, width = residual.shape
+    ff = w_gate.shape[2]
+    half = width // 2
+    cols = half // PROJ_PARTS
+    out_cols = width // 4 // OUT_PARTS
+    all_tokens = 2 * tokens
+    vmem = pl.BlockSpec(memory_space=pltpu.VMEM)
+    hbm = pl.BlockSpec(memory_space=pl.ANY)
+    scratch = [
+        pltpu.VMEM(out_weight.shape, BF),
+        pltpu.VMEM(w_gate.shape[1:], BF),
+        pltpu.VMEM(w_up.shape[1:], BF),
+        pltpu.VMEM(w_down.shape[1:], BF),
+        pltpu.VMEM((2, 2, tokens, HEAD_WIDTH), BF),
+        pltpu.VMEM((2, own_rows, width), F32),
+        pltpu.VMEM((2, own_rows, EXTRA), F32),
+        pltpu.VMEM((tokens, head_cols), BF),
+        pltpu.VMEM((PROJ_PARTS, tokens, cols), BF),
+        pltpu.VMEM((PROJ_PARTS, tokens, cols), BF),
+        pltpu.VMEM((PROJ_PARTS, 2, 4, ROWS, cols), BF),
+        pltpu.VMEM((PROJ_PARTS, 4, ROWS, cols), BF),
+        pltpu.VMEM((PROJ_PARTS, 4, ROWS, cols), BF),
+        pltpu.VMEM((PROJ_PARTS, 3, ROWS, cols), BF),
+        pltpu.VMEM((ROWS, width), F32),
+        pltpu.VMEM((2, own_rows, width), F32),
+        pltpu.VMEM((2, 16, ROWS, half + EXTRA), BF),
+        pltpu.VMEM((2, all_tokens, ff), BF),
+        pltpu.VMEM((OUT_PARTS, all_tokens, out_cols), BF),
+        pltpu.VMEM((OUT_PARTS, all_tokens, out_cols), BF),
+        pltpu.VMEM((OUT_PARTS, 2, 8, ROWS, out_cols), BF),
+        pltpu.VMEM((OUT_PARTS, 8, ROWS, out_cols), BF),
+        pltpu.VMEM((OUT_PARTS, 8, ROWS, out_cols), BF),
+        pltpu.VMEM((OUT_PARTS, 8, ROWS, out_cols), BF),
+        pltpu.VMEM((2, own_rows, width), F32),
+        pltpu.VMEM((own_rows, width), F32),
+        pltpu.SemaphoreType.DMA((16,)),
+        pltpu.SemaphoreType.DMA((96,)),
+        pltpu.SemaphoreType.DMA((96,)),
+    ]
+    flops = 2 * all_tokens * width * ff * 4 + 2 * tokens * head_cols * width
+    return pl.pallas_call(
+        layer_kernel,
+        out_shape=[jax.ShapeDtypeStruct((own_rows, width), BF)] * 2,
+        in_specs=[vmem] * 7 + [hbm] * 4,
+        out_specs=[vmem] * 2,
+        scratch_shapes=scratch,
+        compiler_params=pltpu.CompilerParams(
+            collective_id=0, has_side_effects=True, vmem_limit_bytes=56 * 2**20
+        ),
+        cost_estimate=pl.CostEstimate(
+            flops=flops, bytes_accessed=24 * 2**20, transcendentals=2**18
+        ),
+    )(
+        queries,
+        keys,
+        values,
+        residual,
+        norm_gain.reshape(1, width),
+        expert_ids,
+        expert_gates,
+        out_weight,
+        w_gate,
+        w_up,
+        w_down,
+    )
+
+
 def solution(mesh):
+    one_block = mesh.shape["ctx"] == 2 and mesh.shape["exp"] == 16
     return jax.shard_map(
-        on_device,
+        layer_on_device if one_block else on_device,
         mesh=mesh,
         in_specs=(
             P("ctx", "exp"),

time: 223 us -> 74.6 us (0.33)
  waiting for transfers between devices: 112 us -> 0 us
  Pallas kernels: 0 us -> 70.8 us
  blocking collectives: 56.5 us -> 0 us
  matrix products: 19.4 us -> 0 us
  between operations: 14.3 us -> 0.64 us
  starting transfers between devices: 12 us -> 0 us
  other arithmetic: 3.76 us -> 0 us
    pallas_call x0 -> x1, Pallas kernels: none -> 70.8 us  [layer_on_device(): pl.pallas_call(layer_kernel, out_shape=[jax.ShapeDtypeStruct((own_rows, w...]
    reduce_scatter x1 -> x0, waiting for transfers between devices: 56.8 us -> none  [on_device(): lax.psum_scatter(jnp.dot(heads_done, out_weight, preferred_element_type=j...]
    all_to_all x2 -> x0, blocking collectives: 45.8 us -> none  [the longest x1 31.3 us: on_device(): lax.all_to_all(outgoing, 'exp', split_axis=0, concat_axis=0, tiled=True)]
    all_gather x1 -> x0, waiting for transfers between devices: 32.6 us -> none  [on_device(): lax.all_gather(local_rows, 'ctx', axis=0, tiled=True)]
    all_to_all x1 -> x0, waiting for transfers between devices: 22.9 us -> none  [on_device(): lax.all_to_all(lax.all_to_all(expert_result, 'ctx', split_axis=0, concat_...]
    dot_general x8 -> x0, matrix products: 19.4 us -> none  [the longest x1 5.35 us: expert_hidden(): gate = jnp.dot(rows_block, gate_local, preferred_element_type=jnp.float32)]
    all_gather x1 -> x0, blocking collectives: 10.7 us -> none  [on_device(): lax.all_gather(hidden, 'ctx', axis=1, tiled=True)]
    all_to_all x1 -> x0, starting transfers between devices: 7.97 us -> none  [on_device(): lax.all_to_all(lax.all_to_all(expert_result, 'ctx', split_axis=0, concat_...]
  transfers between devices with their start and end apart: 4 -> 0, of which waited for: 3 -> 0; matrix products, arithmetic and copies ran while one was open for 2% -> 0% of each run, Pallas kernels for 0% -> 0%
where the time goes in v1:
time: 74.6 us; the launch traced here: 74.4 us
  Pallas kernels  70.8 us (95%)
  local copies, waits for them, and re-layouts  2.95 us (4%)
    pallas_call x1, Pallas kernels, layer_on_device(): pl.pallas_call(layer_kernel, out_shape=[jax.ShapeDtypeStruct((own_rows, w...  70.8 us
    unnamed x2, local copies, waits for them, and re-layouts  2.95 us

profile of v1, /device:TPU:1, one launch (start us, length us, event | category | flops | bytes accessed | tf_op | source)
XLA Modules:
  0.0 74.4 jit_solution(12032964912650374646)
XLA Ops:
  0.6 70.8 %shard_map.122 = (bf16[8,4096]{1,0:T(8,128)(2,1)}, bf16[8,4096]{1,0:T(8,128)(2,1)}) custom-call(bf16[128,512]{1,0:T(8,128)(2,1)} %queries.1, bf16[128,512]{1,0:T(8,128)(2,1)} %keys.1, bf16[128,512]{1,0:T(8,128)(2,1)} %values.1, bf16[8,4096]{1,0:T(8,128)(2,1)} %residual.1, f32[1,4096]{1,0:T(1,128)} %bitcast.1, s32[8,8]{1,0:T(8,128)} %expert_ids.1, ...), custom_call_target="tpu_custom_call" | custom-call | flops 6979321856 | bytes 25165824 | tf_op jit(solution)/shard_map/pallas_call | solution.py:558
  71.4 1.5 %copy.15 = bf16[8,4096]{1,0:T(8,128)(2,1)} copy(bf16[8,4096]{1,0:T(8,128)(2,1)} %get-tuple-element.4) | data formatting | bytes 131072
  72.9 1.5 %copy.16 = bf16[8,4096]{1,0:T(8,128)(2,1)} copy(bf16[8,4096]{1,0:T(8,128)(2,1)} %get-tuple-element.5) | data formatting | bytes 131072

commit v2 on v1

--- a/solution.py
+++ b/solution.py
@@ -228,7 +228,7 @@
     width = mixed_out.shape[1]
     half = width // 2
     cols = half // PROJ_PARTS
-    ff = hidden.shape[2]
+    ff = hidden.shape[3]
     ff_cols = ff // FF_PARTS
     out_half = width // 4
     out_cols = out_half // OUT_PARTS
@@ -237,6 +237,7 @@
     def device(yy, zz, xx, kk):
         return (yy, zz * 4 + xx * 2 + kk)
 
+    zs = (z, z + 1 - 2 * (z % 2), (z + 2) % 4, 3 - z)
     other_core = device(y, z, x, 1 - k)
     x_next = device(y, z, 1 - x, k)
     y_next = device(1 - y, z, x, k)
@@ -374,7 +375,7 @@
     gates = jnp.where(gate_lane < 64, gate_high, gates - gate_high).astype(BF)
 
     def block(xx, yy, zz):
-        return (xx * 2 + yy) * 4 + zz
+        return ((zz // 2) * 4 + xx * 2 + yy) * 2 + zz % 2
 
     own = block(x, y, z)
     for side in range(2):
@@ -388,99 +389,145 @@
     y1, x1 = y + k * (1 - 2 * y), x + (1 - k) * (1 - 2 * x)
     y2, x2 = y + (1 - k) * (1 - 2 * y), x + k * (1 - 2 * x)
     first_to, second_to = device(y1, z, x1, k), device(y2, z, x2, k)
-    along_z = [
-        pass_on(own, device(y, (z + dz) % 4, x, k)) for dz in range(1, 4)
-    ]
-    first, second, second_far, cross = [], [], [], []
-    first.append(pass_on(own, first_to))
-    second.append(pass_on(own, second_to))
+    along_z = [pass_on(own, device(y, zs[1], x, k))]
+    first, second, second_far = {}, {}, {}
+    cross = [[], []]
+    first[0] = pass_on(own, first_to)
+    second[0] = pass_on(own, second_to)
+    along_z += [pass_on(own, device(y, zz, x, k)) for zz in zs[2:]]
     mixed_rows[...] = stream.reshape(2, ROWS // 2, width)
     mixed_out[...] = mixed_rows[k].astype(BF)
-    for i in range(1, 4):
+
+    def take_z(i):
         along_z[i - 1].wait_recv()
-        number = block(x, y, (z + 4 - i) % 4)
-        first.append(pass_on(number, first_to))
-        second.append(pass_on(number, second_to))
-        cross.append(pass_on(number, other_core))
-    for i in range(4):
+        number = block(x, y, zs[i])
+        first[i] = pass_on(number, first_to)
+        second[i] = pass_on(number, second_to)
+        cross[i // 2].append(pass_on(number, other_core))
+
+    def take_first(i):
         first[i].wait_recv()
-        number = block(x1, y1, (z + 4 - i) % 4)
-        second_far.append(pass_on(number, second_to))
-        cross.append(pass_on(number, other_core))
-    for i in range(4):
+        number = block(x1, y1, zs[i])
+        second_far[i] = pass_on(number, second_to)
+        cross[i // 2].append(pass_on(number, other_core))
+
+    def take_second(i):
         second[i].wait_recv()
-        cross.append(pass_on(block(x2, y2, (z + 4 - i) % 4), other_core))
-    for i in range(4):
+        cross[i // 2].append(pass_on(block(x2, y2, zs[i]), other_core))
+
+    def take_far(i):
         second_far[i].wait_recv()
-        cross.append(pass_on(block(1 - x, 1 - y, (z + 4 - i) % 4), other_core))
-    weight_copies["wg"].wait()
-    weight_copies["wu"].wait()
-    for copy in cross:
-        copy.wait_recv()
-
-    all_tokens = rows_all.shape[1] * ROWS
-    across = []
-    for part in range(FF_PARTS):
+        cross[i // 2].append(pass_on(block(1 - x, 1 - y, zs[i]), other_core))
+
+    chunk_tokens = tokens
+    chunk_blocks = chunk_tokens // ROWS
+    across = [[], []]
+
+    def chunk_rows(chunk):
+        pair = z // 2 + chunk * (1 - 2 * (z // 2))
+        return pl.ds(pair * chunk_blocks, chunk_blocks)
+
+    def expert_up(chunk, part):
         span = slice(part * ff_cols, (part + 1) * ff_cols)
-        gate = jnp.zeros((all_tokens, ff_cols), F32)
-        upper = jnp.zeros((all_tokens, ff_cols), F32)
+        gate = jnp.zeros((chunk_tokens, ff_cols), F32)
+        upper = jnp.zeros((chunk_tokens, ff_cols), F32)
         for side in range(2):
-            rows = rows_all[side, :, :, :half].reshape(all_tokens, half)
+            rows = rows_all[side, chunk_rows(chunk), :, :half].reshape(chunk_tokens, half)
             depth = slice(side * half, (side + 1) * half)
             gate += jnp.dot(rows, wg[depth, span], preferred_element_type=F32)
             upper += jnp.dot(rows, wu[depth, span], preferred_element_type=F32)
-        hidden[y, :, span] = (gate / (1.0 + jnp.exp(-gate)) * upper).astype(BF)
-        place = hidden.at[y, :, span]
-        across.append(send(place, place, y_next))
-    picked = rows_all[0, :, :, half:].reshape(all_tokens, EXTRA).astype(F32)
-    picked_lane = lax.broadcasted_iota(jnp.int32, picked.shape, 1) % 64
-    share = jnp.sum(jnp.where(picked_lane == e, picked, 0.0), axis=1, keepdims=True)
+        hidden[chunk, y, :, span] = (gate / (1.0 + jnp.exp(-gate)) * upper).astype(BF)
+        place = hidden.at[chunk, y, :, span]
+        across[chunk].append(send(place, place, y_next))
+
+    take_z(1)
+    take_first(0)
+    take_second(0)
+    take_z(2)
+    take_first(1)
+    take_second(1)
+    take_z(3)
+    take_far(0)
+    take_far(1)
+    weight_copies["wg"].wait()
+    weight_copies["wu"].wait()
+    for copy in cross[0]:
+        copy.wait_recv()
+    expert_up(0, 0)
+    take_first(2)
+    take_second(2)
+    for part in range(1, FF_PARTS):
+        expert_up(0, part)
+        if part == 1:
+            take_first(3)
+            take_second(3)
+    take_far(2)
+    take_far(3)
+    for copy in cross[1]:
+        copy.wait_recv()
+    for part in range(FF_PARTS):
+        expert_up(1, part)
+
+    shares = []
+    for chunk in range(2):
+        picked = rows_all[0, chunk_rows(chunk), :, half:].reshape(chunk_tokens, EXTRA).astype(F32)
+        picked_lane = lax.broadcasted_iota(jnp.int32, picked.shape, 1) % 64
+        shares.append(jnp.sum(jnp.where(picked_lane == e, picked, 0.0), axis=1, keepdims=True))
     weight_copies["wd"].wait()
-    for copy in across:
-        copy.wait_recv()
-
-    def down(which, part):
+
+    def down(chunk, which, part):
         place = columns(which, part, out_half, out_cols)
-        result = jnp.dot(hidden[0], wd[:ff, place], preferred_element_type=F32)
-        result += jnp.dot(hidden[1], wd[ff:, place], preferred_element_type=F32)
-        return result * share
-
-    to_core, to_x, to_z = [], [], []
-    for part in range(OUT_PARTS):
-        oc_send[part] = down(1 - k, part).astype(BF)
-        to_core.append(send(oc_send.at[part], oc_recv.at[part], other_core))
-    for part in range(OUT_PARTS):
-        piece = down(k, part)
-        to_core[part].wait_recv()
-        piece = (piece + oc_recv[part].astype(F32)).astype(BF)
-        ox_send[part] = piece.reshape(2, 8, ROWS, out_cols)
-        to_x.append(send(ox_send.at[part, 1 - x], ox_recv.at[part], x_next))
-    for part in range(OUT_PARTS):
-        to_x[part].wait_recv()
-        oz_send[part] = (ox_send[part, x].astype(F32) + ox_recv[part].astype(F32)).astype(BF)
-        for dy in range(2):
-            for dz in range(4):
-                if dy or dz:
-                    yy, zz = (y + dy) % 2, (z + dz) % 4
-                    to_z.append(
-                        send(
-                            oz_send.at[part, yy * 4 + zz],
+        result = jnp.dot(hidden[chunk, 0], wd[:ff, place], preferred_element_type=F32)
+        result += jnp.dot(hidden[chunk, 1], wd[ff:, place], preferred_element_type=F32)
+        return result * shares[chunk]
+
+    to_x, to_z = {}, {}
+
+    def outputs_to_x(chunk):
+        for copy in across[chunk]:
+            copy.wait_recv()
+        to_core = []
+        for part in range(OUT_PARTS):
+            oc_send[chunk, part] = down(chunk, 1 - k, part).astype(BF)
+            to_core.append(send(oc_send.at[chunk, part], oc_recv.at[chunk, part], other_core))
+        for part in range(OUT_PARTS):
+            piece = down(chunk, k, part)
+            to_core[part].wait_recv()
+            piece = (piece + oc_recv[chunk, part].astype(F32)).astype(BF)
+            ox_send[chunk, part] = piece.reshape(2, 2, 2, ROWS, out_cols)
+            to_x[chunk, part] = send(
+                ox_send.at[chunk, part, 1 - x], ox_recv.at[chunk, part], x_next
+            )
+
+    def outputs_to_z(chunk):
+        for part in range(OUT_PARTS):
+            to_x[chunk, part].wait_recv()
+            oz_send[chunk, part] = (
+                ox_send[chunk, part, x].astype(F32) + ox_recv[chunk, part].astype(F32)
+            ).astype(BF)
+            for dy in range(2):
+                for dz in (2 * chunk, 2 * chunk + 1):
+                    if dy or dz:
+                        yy = y + dy * (1 - 2 * y)
+                        to_z[part, dy, dz] = send(
+                            oz_send.at[chunk, part, yy, zs[dz] % 2],
                             oz_recv.at[part, dy * 4 + dz],
-                            device(yy, zz, x, k),
+                            device(yy, zs[dz], x, k),
                         )
-                    )
-                else:
-                    to_z.append(None)
+
+    outputs_to_x(0)
+    outputs_to_z(0)
+    outputs_to_x(1)
+    outputs_to_z(1)
     back = []
     for part in range(OUT_PARTS):
         for dy in range(2):
             piece = None
             for dz in range(4):
-                copy = to_z[part * 8 + dy * 4 + dz]
-                if copy is None:
-                    piece = oz_send[part, y * 4 + z].astype(F32)
+                if (part, dy, dz) not in to_z:
+                    piece = oz_send[0, part, y, z % 2].astype(F32)
                     continue
-                copy.wait_recv()
+                to_z[part, dy, dz].wait_recv()
                 came = oz_recv[part, dy * 4 + dz].astype(F32)
                 piece = came if piece is None else piece + came
             side = y + dy * (1 - 2 * y)
@@ -541,12 +588,12 @@
         pltpu.VMEM((ROWS, width), F32),
         pltpu.VMEM((2, own_rows, width), F32),
         pltpu.VMEM((2, 16, ROWS, half + EXTRA), BF),
-        pltpu.VMEM((2, all_tokens, ff), BF),
-        pltpu.VMEM((OUT_PARTS, all_tokens, out_cols), BF),
-        pltpu.VMEM((OUT_PARTS, all_tokens, out_cols), BF),
-        pltpu.VMEM((OUT_PARTS, 2, 8, ROWS, out_cols), BF),
-        pltpu.VMEM((OUT_PARTS, 8, ROWS, out_cols), BF),
-        pltpu.VMEM((OUT_PARTS, 8, ROWS, out_cols), BF),
+        pltpu.VMEM((2, 2, tokens, ff), BF),
+        pltpu.VMEM((2, OUT_PARTS, tokens, out_cols), BF),
+        pltpu.VMEM((2, OUT_PARTS, tokens, out_cols), BF),
+        pltpu.VMEM((2, OUT_PARTS, 2, 2, 2, ROWS, out_cols), BF),
+        pltpu.VMEM((2, OUT_PARTS, 2, 2, ROWS, out_cols), BF),
+        pltpu.VMEM((2, OUT_PARTS, 2, 2, ROWS, out_cols), BF),
         pltpu.VMEM((OUT_PARTS, 8, ROWS, out_cols), BF),
         pltpu.VMEM((2, own_rows, width), F32),
         pltpu.VMEM((own_rows, width), F32),

time: 74.6 us -> 75.2 us (level)
  no operation moved by 1% of the time
where the time goes in v2:
time: 75.2 us; the launch traced here: 75 us
  Pallas kernels  71.4 us (95%)
  local copies, waits for them, and re-layouts  2.95 us (4%)
    pallas_call x1, Pallas kernels, layer_on_device(): pl.pallas_call(layer_kernel, out_shape=[jax.ShapeDtypeStruct((own_rows, w...  71.4 us
    unnamed x2, local copies, waits for them, and re-layouts  2.95 us

profile of v2, /device:TPU:1, one launch (start us, length us, event | category | flops | bytes accessed | tf_op | source)
XLA Modules:
  0.0 75.0 jit_solution(1671889908411889111)
XLA Ops:
  0.6 71.4 %shard_map.122 = (bf16[8,4096]{1,0:T(8,128)(2,1)}, bf16[8,4096]{1,0:T(8,128)(2,1)}) custom-call(bf16[128,512]{1,0:T(8,128)(2,1)} %queries.1, bf16[128,512]{1,0:T(8,128)(2,1)} %keys.1, bf16[128,512]{1,0:T(8,128)(2,1)} %values.1, bf16[8,4096]{1,0:T(8,128)(2,1)} %residual.1, f32[1,4096]{1,0:T(1,128)} %bitcast.1, s32[8,8]{1,0:T(8,128)} %expert_ids.1, ...), custom_call_target="tpu_custom_call" | custom-call | flops 6979321856 | bytes 25165824 | tf_op jit(solution)/shard_map/pallas_call | solution.py:605
  72.1 1.5 %copy.15 = bf16[8,4096]{1,0:T(8,128)(2,1)} copy(bf16[8,4096]{1,0:T(8,128)(2,1)} %get-tuple-element.4) | data formatting | bytes 131072
  73.5 1.5 %copy.16 = bf16[8,4096]{1,0:T(8,128)(2,1)} copy(bf16[8,4096]{1,0:T(8,128)(2,1)} %get-tuple-element.5) | data formatting | bytes 131072

commit v3 on v2

--- a/solution.py
+++ b/solution.py
@@ -294,9 +294,6 @@
     kv_copy = send(kv.at[y], kv.at[y], y_next)
     res_copy = send(res.at[k], res.at[k], other_core)
     table_copy = send(table.at[k], table.at[k], other_core)
-    fetch("wg", wg_hbm.at[0], wg)
-    fetch("wu", wu_hbm.at[0], wu)
-    fetch("wd", wd_hbm.at[0], wd)
 
     kv_copy.wait_recv()
     key_all = kv[:, 0].reshape(2 * tokens, HEAD_WIDTH)
@@ -333,6 +330,7 @@
         )
         pc_send[part] = piece.astype(BF)
         to_core.append(send(pc_send.at[part], pc_recv.at[part], other_core))
+    fetch("wg", wg_hbm.at[0], wg)
     to_x = []
     for part in range(PROJ_PARTS):
         piece = jnp.dot(
@@ -343,6 +341,7 @@
         for chip in range(tokens // ROWS):
             px_send[part, chip % 2, chip // 2] = piece[chip * ROWS : (chip + 1) * ROWS]
         to_x.append(send(px_send.at[part, 1 - x], px_recv.at[part], x_next))
+    fetch("wu", wu_hbm.at[0], wu)
     to_z = []
     for part in range(PROJ_PARTS):
         to_x[part].wait_recv()
@@ -352,6 +351,7 @@
             to_z.append(
                 send(pz_send.at[part, zz], pz_recv.at[part, dz - 1], device(y, zz, x, k))
             )
+    fetch("wd", wd_hbm.at[0], wd)
     back = []
     for part in range(PROJ_PARTS):
         piece = pz_send[part, z].astype(F32)
@@ -483,13 +483,16 @@
 
     to_x, to_z = {}, {}
 
-    def outputs_to_x(chunk):
+    def outputs_to_core(chunk):
         for copy in across[chunk]:
             copy.wait_recv()
         to_core = []
         for part in range(OUT_PARTS):
             oc_send[chunk, part] = down(chunk, 1 - k, part).astype(BF)
             to_core.append(send(oc_send.at[chunk, part], oc_recv.at[chunk, part], other_core))
+        return to_core
+
+    def outputs_to_x(chunk, to_core):
         for part in range(OUT_PARTS):
             piece = down(chunk, k, part)
             to_core[part].wait_recv()
@@ -515,9 +518,10 @@
                             device(yy, zs[dz], x, k),
                         )
 
-    outputs_to_x(0)
+    outputs_to_x(0, outputs_to_core(0))
+    to_core = outputs_to_core(1)
     outputs_to_z(0)
-    outputs_to_x(1)
+    outputs_to_x(1, to_core)
     outputs_to_z(1)
     back = []
     for part in range(OUT_PARTS):
@@ -546,6 +550,15 @@
             experts_out[:, place] = eo_recv[:, place].astype(BF)
     for copy in sent:
         copy.wait_send()
+
+
+def hand_over(mixed, experts, mixed_out, experts_out, sems):
+    first = pltpu.make_async_copy(mixed, mixed_out, sems.at[0])
+    second = pltpu.make_async_copy(experts, experts_out, sems.at[1])
+    first.start()
+    second.start()
+    first.wait()
+    second.wait()
 
 
 def layer_on_device(
@@ -602,7 +615,7 @@
         pltpu.SemaphoreType.DMA((96,)),
     ]
     flops = 2 * all_tokens * width * ff * 4 + 2 * tokens * head_cols * width
-    return pl.pallas_call(
+    mixed, experts = pl.pallas_call(
         layer_kernel,
         out_shape=[jax.ShapeDtypeStruct((own_rows, width), BF)] * 2,
         in_specs=[vmem] * 7 + [hbm] * 4,
@@ -627,6 +640,15 @@
         w_up,
         w_down,
     )
+    return tuple(
+        pl.pallas_call(
+            hand_over,
+            out_shape=[jax.ShapeDtypeStruct((own_rows, width), BF)] * 2,
+            in_specs=[hbm] * 2,
+            out_specs=[hbm] * 2,
+            scratch_shapes=[pltpu.SemaphoreType.DMA((2,))],
+        )(mixed, experts)
+    )
 
 
 def solution(mesh):

time: 75.2 us -> 74.8 us (level)
  local copies, waits for them, and re-layouts: 2.95 us -> 0 us
  Pallas kernels: 71.4 us -> 74 us
    pallas_call x0 -> x1, Pallas kernels: none -> 5.09 us  [layer_on_device(): pl.pallas_call(hand_over, out_shape=[jax.ShapeDtypeStruct((own_rows, widt...]
    unnamed x2 -> x0, local copies, waits for them, and re-layouts: 2.95 us -> none
    pallas_call x1, Pallas kernels: 71.4 us -> 68.9 us  [layer_on_device(): pl.pallas_call(layer_kernel, out_shape=[jax.ShapeDtypeStruct((own_rows, w...]
where the time goes in v3:
time: 74.8 us; the launch traced here: 74.6 us
  Pallas kernels  74 us (99%)
    pallas_call x1, Pallas kernels, layer_on_device(): pl.pallas_call(layer_kernel, out_shape=[jax.ShapeDtypeStruct((own_rows, w...  68.9 us
    pallas_call x1, Pallas kernels, layer_on_device(): pl.pallas_call(hand_over, out_shape=[jax.ShapeDtypeStruct((own_rows, widt...  5.09 us

profile of v3, /device:TPU:1, one launch (start us, length us, event | category | flops | bytes accessed | tf_op | source)
XLA Modules:
  0.0 74.6 jit_solution(10188251070816825521)
XLA Ops:
  0.6 68.9 %shard_map.122 = (bf16[8,4096]{1,0:T(8,128)(2,1)}, bf16[8,4096]{1,0:T(8,128)(2,1)}) custom-call(bf16[128,512]{1,0:T(8,128)(2,1)} %queries.1, bf16[128,512]{1,0:T(8,128)(2,1)} %keys.1, bf16[128,512]{1,0:T(8,128)(2,1)} %values.1, bf16[8,4096]{1,0:T(8,128)(2,1)} %residual.1, f32[1,4096]{1,0:T(1,128)} %bitcast.1, s32[8,8]{1,0:T(8,128)} %expert_ids.1, ...), custom_call_target="tpu_custom_call" | custom-call | flops 6979321856 | bytes 25165824 | tf_op jit(solution)/shard_map/pallas_call | solution.py:618
  69.5 5.1 %shard_map.123 = (bf16[8,4096]{1,0:T(8,128)(2,1)}, bf16[8,4096]{1,0:T(8,128)(2,1)}) custom-call(bf16[8,4096]{1,0:T(8,128)(2,1)} %get-tuple-element.4.mixed, bf16[8,4096]{1,0:T(8,128)(2,1)} %get-tuple-element.5.experts), custom_call_target="tpu_custom_call" | custom-call | tf_op jit(solution)/shard_map/pallas_call | solution.py:644

commit v4 on v1

--- a/solution.py
+++ b/solution.py
@@ -173,9 +173,9 @@
 F32 = jnp.float32
 ROWS = 16
 EXTRA = 128
-PROJ_PARTS = 4
+PROJ_PARTS = 8
 FF_PARTS = 3
-OUT_PARTS = 2
+OUT_PARTS = 4
 
 
 def layer_kernel(
@@ -190,8 +190,7 @@
     wg_hbm,
     wu_hbm,
     wd_hbm,
-    mixed_out,
-    experts_out,
+    results,
     wo,
     wg,
     wu,
@@ -218,6 +217,7 @@
     oz_recv,
     eo,
     eo_recv,
+    own_down,
     w_sem,
     send_sem,
     recv_sem,
@@ -225,7 +225,7 @@
     y = lax.axis_index("ctx")
     e = lax.axis_index("exp")
     z, x, k = e // 4, (e // 2) % 2, e % 2
-    width = mixed_out.shape[1]
+    width = residual.shape[1]
     half = width // 2
     cols = half // PROJ_PARTS
     ff = hidden.shape[2]
@@ -293,9 +293,6 @@
     kv_copy = send(kv.at[y], kv.at[y], y_next)
     res_copy = send(res.at[k], res.at[k], other_core)
     table_copy = send(table.at[k], table.at[k], other_core)
-    fetch("wg", wg_hbm.at[0], wg)
-    fetch("wu", wu_hbm.at[0], wu)
-    fetch("wd", wd_hbm.at[0], wd)
 
     kv_copy.wait_recv()
     key_all = kv[:, 0].reshape(2 * tokens, HEAD_WIDTH)
@@ -332,6 +329,7 @@
         )
         pc_send[part] = piece.astype(BF)
         to_core.append(send(pc_send.at[part], pc_recv.at[part], other_core))
+    fetch("wg", wg_hbm.at[0], wg)
     to_x = []
     for part in range(PROJ_PARTS):
         piece = jnp.dot(
@@ -342,6 +340,7 @@
         for chip in range(tokens // ROWS):
             px_send[part, chip % 2, chip // 2] = piece[chip * ROWS : (chip + 1) * ROWS]
         to_x.append(send(px_send.at[part, 1 - x], px_recv.at[part], x_next))
+    fetch("wu", wu_hbm.at[0], wu)
     to_z = []
     for part in range(PROJ_PARTS):
         to_x[part].wait_recv()
@@ -351,6 +350,7 @@
             to_z.append(
                 send(pz_send.at[part, zz], pz_recv.at[part, dz - 1], device(y, zz, x, k))
             )
+    fetch("wd", wd_hbm.at[0], wd)
     back = []
     for part in range(PROJ_PARTS):
         piece = pz_send[part, z].astype(F32)
@@ -395,7 +395,7 @@
     first.append(pass_on(own, first_to))
     second.append(pass_on(own, second_to))
     mixed_rows[...] = stream.reshape(2, ROWS // 2, width)
-    mixed_out[...] = mixed_rows[k].astype(BF)
+    results[0] = mixed_rows[k].astype(BF)
     for i in range(1, 4):
         along_z[i - 1].wait_recv()
         number = block(x, y, (z + 4 - i) % 4)
@@ -436,14 +436,20 @@
     picked_lane = lax.broadcasted_iota(jnp.int32, picked.shape, 1) % 64
     share = jnp.sum(jnp.where(picked_lane == e, picked, 0.0), axis=1, keepdims=True)
     weight_copies["wd"].wait()
+    own_depth = pl.ds(pl.multiple_of(y * ff, ff), ff)
+    far_depth = pl.ds(pl.multiple_of((1 - y) * ff, ff), ff)
+    for which in range(2 * OUT_PARTS):
+        span = slice(which * out_cols, (which + 1) * out_cols)
+        own_down[which] = jnp.dot(
+            hidden[y], wd[own_depth, span], preferred_element_type=F32
+        )
     for copy in across:
         copy.wait_recv()
 
     def down(which, part):
         place = columns(which, part, out_half, out_cols)
-        result = jnp.dot(hidden[0], wd[:ff, place], preferred_element_type=F32)
-        result += jnp.dot(hidden[1], wd[ff:, place], preferred_element_type=F32)
-        return result * share
+        result = jnp.dot(hidden[1 - y], wd[far_depth, place], preferred_element_type=F32)
+        return (result + own_down[which * OUT_PARTS + part]) * share
 
     to_core, to_x, to_z = [], [], []
     for part in range(OUT_PARTS):
@@ -490,13 +496,13 @@
     for part in range(OUT_PARTS):
         for side in range(2):
             place = columns(side * 2 + k, part, out_half, out_cols)
-            experts_out[:, place] = eo[k, :, place].astype(BF)
+            results[1, :, place] = eo[k, :, place].astype(BF)
     for copy in back:
         copy.wait_recv()
     for part in range(OUT_PARTS):
         for side in range(2):
             place = columns(side * 2 + 1 - k, part, out_half, out_cols)
-            experts_out[:, place] = eo_recv[:, place].astype(BF)
+            results[1, :, place] = eo_recv[:, place].astype(BF)
     for copy in sent:
         copy.wait_send()
 
@@ -550,16 +556,17 @@
         pltpu.VMEM((OUT_PARTS, 8, ROWS, out_cols), BF),
         pltpu.VMEM((2, own_rows, width), F32),
         pltpu.VMEM((own_rows, width), F32),
+        pltpu.VMEM((2 * OUT_PARTS, all_tokens, out_cols), F32),
         pltpu.SemaphoreType.DMA((16,)),
-        pltpu.SemaphoreType.DMA((96,)),
-        pltpu.SemaphoreType.DMA((96,)),
+        pltpu.SemaphoreType.DMA((136,)),
+        pltpu.SemaphoreType.DMA((136,)),
     ]
     flops = 2 * all_tokens * width * ff * 4 + 2 * tokens * head_cols * width
-    return pl.pallas_call(
+    results = pl.pallas_call(
         layer_kernel,
-        out_shape=[jax.ShapeDtypeStruct((own_rows, width), BF)] * 2,
+        out_shape=jax.ShapeDtypeStruct((2, own_rows, width), BF),
         in_specs=[vmem] * 7 + [hbm] * 4,
-        out_specs=[vmem] * 2,
+        out_specs=vmem,
         scratch_shapes=scratch,
         compiler_params=pltpu.CompilerParams(
             collective_id=0, has_side_effects=True, vmem_limit_bytes=56 * 2**20
@@ -580,6 +587,7 @@
         w_up,
         w_down,
     )
+    return results[0], results[1]
 
 
 def solution(mesh):

time: 74.6 us -> 73 us (0.979)
  local copies, waits for them, and re-layouts: 2.95 us -> 1.53 us
    unnamed x2 -> x0, local copies, waits for them, and re-layouts: 2.95 us -> none
    squeeze x0 -> x1, local copies, waits for them, and re-layouts: none -> 1.53 us  [layer_on_device(): return (results[0], results[1])]
where the time goes in v4:
time: 73 us; the launch traced here: 72.9 us
  Pallas kernels  70.7 us (97%)
  local copies, waits for them, and re-layouts  1.53 us (2%)
    pallas_call x1, Pallas kernels, layer_on_device(): pl.pallas_call(layer_kernel, out_shape=jax.ShapeDtypeStruct((2, own_rows,...  70.7 us
    squeeze x1, local copies, waits for them, and re-layouts, layer_on_device(): return (results[0], results[1])  1.53 us

profile of v4, /device:TPU:1, one launch (start us, length us, event | category | flops | bytes accessed | tf_op | source)
XLA Modules:
  0.0 72.9 jit_solution(1906960716739047384)
XLA Ops:
  0.6 70.7 %shard_map.122 = bf16[2,8,4096]{2,1,0:T(8,128)(2,1)} custom-call(bf16[128,512]{1,0:T(8,128)(2,1)} %queries.1, bf16[128,512]{1,0:T(8,128)(2,1)} %keys.1, bf16[128,512]{1,0:T(8,128)(2,1)} %values.1, bf16[8,4096]{1,0:T(8,128)(2,1)} %residual.1, f32[1,4096]{1,0:T(1,128)} %bitcast.5, s32[8,8]{1,0:T(8,128)} %expert_ids.1, f32[8,8]{1,0:T(8,128)} %expert_gates.1, ...), custom_call_target="tpu_custom_call" | custom-call | flops 6979321856 | bytes 25165824 | tf_op jit(solution)/shard_map/pallas_call | solution.py:565
  71.3 1.5 %slice_bitcast_fusion = (bf16[8,4096]{1,0:T(8,128)(2,1)}, bf16[8,4096]{1,0:T(8,128)(2,1)}) fusion(bf16[2,8,4096]{2,1,0:T(8,128)(2,1)} %shard_map.122), kind=kLoop, calls=%fused_computation | loop fusion | bytes 262144 | tf_op jit(solution)/shard_map/squeeze | solution.py:590

commit v5 on v4

--- a/solution.py
+++ b/solution.py
@@ -173,9 +173,9 @@
 F32 = jnp.float32
 ROWS = 16
 EXTRA = 128
-PROJ_PARTS = 8
+PROJ_PARTS = 2
 FF_PARTS = 3
-OUT_PARTS = 4
+OUT_PARTS = 2
 
 
 def layer_kernel(
@@ -377,42 +377,44 @@
         return (xx * 2 + yy) * 4 + zz
 
     own = block(x, y, z)
-    for side in range(2):
-        rows_all[side, own, :, :half] = normed[:, side * half : (side + 1) * half]
-        rows_all[side, own, :, half:] = gates
-
-    def pass_on(number, to):
-        place = rows_all.at[k, number]
+    side_rows = jnp.where(k == 0, normed[:, :half], normed[:, half:])
+    rows_all[k, own, :, :half] = side_rows
+    rows_all[k, own, :, half:] = gates
+
+    def pass_on(number, count, to):
+        place = rows_all.at[k, pl.ds(number, count)]
         return send(place, place, to)
 
     y1, x1 = y + k * (1 - 2 * y), x + (1 - k) * (1 - 2 * x)
     y2, x2 = y + (1 - k) * (1 - 2 * y), x + k * (1 - 2 * x)
     first_to, second_to = device(y1, z, x1, k), device(y2, z, x2, k)
-    along_z = [
-        pass_on(own, device(y, (z + dz) % 4, x, k)) for dz in range(1, 4)
-    ]
-    first, second, second_far, cross = [], [], [], []
-    first.append(pass_on(own, first_to))
-    second.append(pass_on(own, second_to))
+    zs = (z, z + 1 - 2 * (z % 2), (z + 2) % 4, 3 - z)
+    along_z = [pass_on(own, 1, device(y, zz, x, k)) for zz in zs[1:]]
     mixed_rows[...] = stream.reshape(2, ROWS // 2, width)
     results[0] = mixed_rows[k].astype(BF)
-    for i in range(1, 4):
-        along_z[i - 1].wait_recv()
-        number = block(x, y, (z + 4 - i) % 4)
-        first.append(pass_on(number, first_to))
-        second.append(pass_on(number, second_to))
-        cross.append(pass_on(number, other_core))
-    for i in range(4):
+    pairs = ((z // 2) * 2, 2 - (z // 2) * 2)
+    first, second, second_far, cross = [], [], [], []
+    for i in range(2):
+        if i == 0:
+            along_z[0].wait_recv()
+        else:
+            along_z[1].wait_recv()
+            along_z[2].wait_recv()
+        number = block(x, y, pairs[i])
+        first.append(pass_on(number, 2, first_to))
+        second.append(pass_on(number, 2, second_to))
+        cross.append(pass_on(number, 2, other_core))
+    for i in range(2):
         first[i].wait_recv()
-        number = block(x1, y1, (z + 4 - i) % 4)
-        second_far.append(pass_on(number, second_to))
-        cross.append(pass_on(number, other_core))
-    for i in range(4):
+        number = block(x1, y1, pairs[i])
+        second_far.append(pass_on(number, 2, second_to))
+        cross.append(pass_on(number, 2, other_core))
+    for i in range(2):
         second[i].wait_recv()
-        cross.append(pass_on(block(x2, y2, (z + 4 - i) % 4), other_core))
-    for i in range(4):
+        cross.append(pass_on(block(x2, y2, pairs[i]), 2, other_core))
+    for i in range(2):
         second_far[i].wait_recv()
-        cross.append(pass_on(block(1 - x, 1 - y, (z + 4 - i) % 4), other_core))
+        cross.append(pass_on(block(1 - x, 1 - y, pairs[i]), 2, other_core))
     weight_copies["wg"].wait()
     weight_copies["wu"].wait()
     for copy in cross:

time: 73 us -> 76.5 us (1.048)
  Pallas kernels: 70.7 us -> 74.1 us
    pallas_call x1, Pallas kernels: 70.7 us -> 74.1 us  [layer_on_device(): pl.pallas_call(layer_kernel, out_shape=jax.ShapeDtypeStruct((2, own_rows,...]
where the time goes in v5:
time: 76.5 us; the launch traced here: 76.3 us
  Pallas kernels  74.1 us (97%)
  local copies, waits for them, and re-layouts  1.53 us (2%)
    pallas_call x1, Pallas kernels, layer_on_device(): pl.pallas_call(layer_kernel, out_shape=jax.ShapeDtypeStruct((2, own_rows,...  74.1 us

profile of v5, /device:TPU:1, one launch (start us, length us, event | category | flops | bytes accessed | tf_op | source)
XLA Modules:
  0.0 76.3 jit_solution(8613468062404566845)
XLA Ops:
  0.6 74.1 %shard_map.122 = bf16[2,8,4096]{2,1,0:T(8,128)(2,1)} custom-call(bf16[128,512]{1,0:T(8,128)(2,1)} %queries.1, bf16[128,512]{1,0:T(8,128)(2,1)} %keys.1, bf16[128,512]{1,0:T(8,128)(2,1)} %values.1, bf16[8,4096]{1,0:T(8,128)(2,1)} %residual.1, f32[1,4096]{1,0:T(1,128)} %bitcast.5, s32[8,8]{1,0:T(8,128)} %expert_ids.1, f32[8,8]{1,0:T(8,128)} %expert_gates.1, ...), custom_call_target="tpu_custom_call" | custom-call | flops 6979321856 | bytes 25165824 | tf_op jit(solution)/shard_map/pallas_call | solution.py:567
  74.8 1.5 %slice_bitcast_fusion = (bf16[8,4096]{1,0:T(8,128)(2,1)}, bf16[8,4096]{1,0:T(8,128)(2,1)}) fusion(bf16[2,8,4096]{2,1,0:T(8,128)(2,1)} %shard_map.122), kind=kLoop, calls=%fused_computation | loop fusion | bytes 262144 | tf_op jit(solution)/shard_map/squeeze | solution.py:592

commit v6 on v2

--- a/solution.py
+++ b/solution.py
@@ -190,8 +190,7 @@
     wg_hbm,
     wu_hbm,
     wd_hbm,
-    mixed_out,
-    experts_out,
+    results,
     wo,
     wg,
     wu,
@@ -218,6 +217,7 @@
     oz_recv,
     eo,
     eo_recv,
+    own_down,
     w_sem,
     send_sem,
     recv_sem,
@@ -225,7 +225,7 @@
     y = lax.axis_index("ctx")
     e = lax.axis_index("exp")
     z, x, k = e // 4, (e // 2) % 2, e % 2
-    width = mixed_out.shape[1]
+    width = residual.shape[1]
     half = width // 2
     cols = half // PROJ_PARTS
     ff = hidden.shape[3]
@@ -294,9 +294,6 @@
     kv_copy = send(kv.at[y], kv.at[y], y_next)
     res_copy = send(res.at[k], res.at[k], other_core)
     table_copy = send(table.at[k], table.at[k], other_core)
-    fetch("wg", wg_hbm.at[0], wg)
-    fetch("wu", wu_hbm.at[0], wu)
-    fetch("wd", wd_hbm.at[0], wd)
 
     kv_copy.wait_recv()
     key_all = kv[:, 0].reshape(2 * tokens, HEAD_WIDTH)
@@ -333,6 +330,7 @@
         )
         pc_send[part] = piece.astype(BF)
         to_core.append(send(pc_send.at[part], pc_recv.at[part], other_core))
+    fetch("wg", wg_hbm.at[0], wg)
     to_x = []
     for part in range(PROJ_PARTS):
         piece = jnp.dot(
@@ -343,6 +341,7 @@
         for chip in range(tokens // ROWS):
             px_send[part, chip % 2, chip // 2] = piece[chip * ROWS : (chip + 1) * ROWS]
         to_x.append(send(px_send.at[part, 1 - x], px_recv.at[part], x_next))
+    fetch("wu", wu_hbm.at[0], wu)
     to_z = []
     for part in range(PROJ_PARTS):
         to_x[part].wait_recv()
@@ -352,6 +351,7 @@
             to_z.append(
                 send(pz_send.at[part, zz], pz_recv.at[part, dz - 1], device(y, zz, x, k))
             )
+    fetch("wd", wd_hbm.at[0], wd)
     back = []
     for part in range(PROJ_PARTS):
         piece = pz_send[part, z].astype(F32)
@@ -396,7 +396,7 @@
     second[0] = pass_on(own, second_to)
     along_z += [pass_on(own, device(y, zz, x, k)) for zz in zs[2:]]
     mixed_rows[...] = stream.reshape(2, ROWS // 2, width)
-    mixed_out[...] = mixed_rows[k].astype(BF)
+    results[0] = mixed_rows[k].astype(BF)
 
     def take_z(i):
         along_z[i - 1].wait_recv()
@@ -475,21 +475,37 @@
         shares.append(jnp.sum(jnp.where(picked_lane == e, picked, 0.0), axis=1, keepdims=True))
     weight_copies["wd"].wait()
 
+    own_depth = pl.ds(pl.multiple_of(y * ff, ff), ff)
+    far_depth = pl.ds(pl.multiple_of((1 - y) * ff, ff), ff)
+
+    def down_own(chunk):
+        for which in range(2 * OUT_PARTS):
+            span = slice(which * out_cols, (which + 1) * out_cols)
+            own_down[which] = jnp.dot(
+                hidden[chunk, y], wd[own_depth, span], preferred_element_type=F32
+            )
+
     def down(chunk, which, part):
         place = columns(which, part, out_half, out_cols)
-        result = jnp.dot(hidden[chunk, 0], wd[:ff, place], preferred_element_type=F32)
-        result += jnp.dot(hidden[chunk, 1], wd[ff:, place], preferred_element_type=F32)
+        result = jnp.dot(hidden[chunk, 1 - y], wd[far_depth, place], preferred_element_type=F32)
+        if chunk:
+            result += own_down[which * OUT_PARTS + part]
+        else:
+            result += jnp.dot(hidden[chunk, y], wd[own_depth, place], preferred_element_type=F32)
         return result * shares[chunk]
 
     to_x, to_z = {}, {}
 
-    def outputs_to_x(chunk):
+    def outputs_to_core(chunk):
         for copy in across[chunk]:
             copy.wait_recv()
         to_core = []
         for part in range(OUT_PARTS):
             oc_send[chunk, part] = down(chunk, 1 - k, part).astype(BF)
             to_core.append(send(oc_send.at[chunk, part], oc_recv.at[chunk, part], other_core))
+        return to_core
+
+    def outputs_to_x(chunk, to_core):
         for part in range(OUT_PARTS):
             piece = down(chunk, k, part)
             to_core[part].wait_recv()
@@ -515,9 +531,11 @@
                             device(yy, zs[dz], x, k),
                         )
 
-    outputs_to_x(0)
+    outputs_to_x(0, outputs_to_core(0))
+    down_own(1)
+    to_core = outputs_to_core(1)
     outputs_to_z(0)
-    outputs_to_x(1)
+    outputs_to_x(1, to_core)
     outputs_to_z(1)
     back = []
     for part in range(OUT_PARTS):
@@ -537,13 +555,13 @@
     for part in range(OUT_PARTS):
         for side in range(2):
             place = columns(side * 2 + k, part, out_half, out_cols)
-            experts_out[:, place] = eo[k, :, place].astype(BF)
+            results[1, :, place] = eo[k, :, place].astype(BF)
     for copy in back:
         copy.wait_recv()
     for part in range(OUT_PARTS):
         for side in range(2):
             place = columns(side * 2 + 1 - k, part, out_half, out_cols)
-            experts_out[:, place] = eo_recv[:, place].astype(BF)
+            results[1, :, place] = eo_recv[:, place].astype(BF)
     for copy in sent:
         copy.wait_send()
 
@@ -597,16 +615,17 @@
         pltpu.VMEM((OUT_PARTS, 8, ROWS, out_cols), BF),
         pltpu.VMEM((2, own_rows, width), F32),
         pltpu.VMEM((own_rows, width), F32),
+        pltpu.VMEM((2 * OUT_PARTS, tokens, out_cols), F32),
         pltpu.SemaphoreType.DMA((16,)),
         pltpu.SemaphoreType.DMA((96,)),
         pltpu.SemaphoreType.DMA((96,)),
     ]
     flops = 2 * all_tokens * width * ff * 4 + 2 * tokens * head_cols * width
-    return pl.pallas_call(
+    results = pl.pallas_call(
         layer_kernel,
-        out_shape=[jax.ShapeDtypeStruct((own_rows, width), BF)] * 2,
+        out_shape=jax.ShapeDtypeStruct((2, own_rows, width), BF),
         in_specs=[vmem] * 7 + [hbm] * 4,
-        out_specs=[vmem] * 2,
+        out_specs=vmem,
         scratch_shapes=scratch,
         compiler_params=pltpu.CompilerParams(
             collective_id=0, has_side_effects=True, vmem_limit_bytes=56 * 2**20
@@ -627,6 +646,7 @@
         w_up,
         w_down,
     )
+    return results[0], results[1]
 
 
 def solution(mesh):

time: 75.2 us -> 71.1 us (0.945)
  Pallas kernels: 71.4 us -> 68.8 us
  local copies, waits for them, and re-layouts: 2.95 us -> 1.53 us
    unnamed x2 -> x0, local copies, waits for them, and re-layouts: 2.95 us -> none
    pallas_call x1, Pallas kernels: 71.4 us -> 68.8 us  [layer_on_device(): pl.pallas_call(layer_kernel, out_shape=jax.ShapeDtypeStruct((2, own_rows,...]
    squeeze x0 -> x1, local copies, waits for them, and re-layouts: none -> 1.53 us  [layer_on_device(): return (results[0], results[1])]
where the time goes in v6:
time: 71.1 us; the launch traced here: 71 us
  Pallas kernels  68.8 us (97%)
  local copies, waits for them, and re-layouts  1.53 us (2%)
    pallas_call x1, Pallas kernels, layer_on_device(): pl.pallas_call(layer_kernel, out_shape=jax.ShapeDtypeStruct((2, own_rows,...  68.8 us
    squeeze x1, local copies, waits for them, and re-layouts, layer_on_device(): return (results[0], results[1])  1.53 us

profile of v6, /device:TPU:1, one launch (start us, length us, event | category | flops | bytes accessed | tf_op | source)
XLA Modules:
  0.0 71.0 jit_solution(8687310247412174081)
XLA Ops:
  0.6 68.8 %shard_map.122 = bf16[2,8,4096]{2,1,0:T(8,128)(2,1)} custom-call(bf16[128,512]{1,0:T(8,128)(2,1)} %queries.1, bf16[128,512]{1,0:T(8,128)(2,1)} %keys.1, bf16[128,512]{1,0:T(8,128)(2,1)} %values.1, bf16[8,4096]{1,0:T(8,128)(2,1)} %residual.1, f32[1,4096]{1,0:T(1,128)} %bitcast.5, s32[8,8]{1,0:T(8,128)} %expert_ids.1, f32[8,8]{1,0:T(8,128)} %expert_gates.1, ...), custom_call_target="tpu_custom_call" | custom-call | flops 6979321856 | bytes 25165824 | tf_op jit(solution)/shard_map/pallas_call | solution.py:624
  69.4 1.5 %slice_bitcast_fusion = (bf16[8,4096]{1,0:T(8,128)(2,1)}, bf16[8,4096]{1,0:T(8,128)(2,1)}) fusion(bf16[2,8,4096]{2,1,0:T(8,128)(2,1)} %shard_map.122), kind=kLoop, calls=%fused_computation | loop fusion | bytes 262144 | tf_op jit(solution)/shard_map/squeeze | solution.py:649

commit v7 on v6

--- a/solution.py
+++ b/solution.py
@@ -173,7 +173,7 @@
 F32 = jnp.float32
 ROWS = 16
 EXTRA = 128
-PROJ_PARTS = 4
+PROJ_PARTS = 8
 FF_PARTS = 3
 OUT_PARTS = 2
 
@@ -617,8 +617,8 @@
         pltpu.VMEM((own_rows, width), F32),
         pltpu.VMEM((2 * OUT_PARTS, tokens, out_cols), F32),
         pltpu.SemaphoreType.DMA((16,)),
-        pltpu.SemaphoreType.DMA((96,)),
-        pltpu.SemaphoreType.DMA((96,)),
+        pltpu.SemaphoreType.DMA((128,)),
+        pltpu.SemaphoreType.DMA((128,)),
     ]
     flops = 2 * all_tokens * width * ff * 4 + 2 * tokens * head_cols * width
     results = pl.pallas_call(

time: 71.1 us -> 71.3 us (level)
  no operation moved by 1% of the time
where the time goes in v7:
time: 71.3 us; the launch traced here: 71.1 us
  Pallas kernels  69 us (97%)
  local copies, waits for them, and re-layouts  1.53 us (2%)
    pallas_call x1, Pallas kernels, layer_on_device(): pl.pallas_call(layer_kernel, out_shape=jax.ShapeDtypeStruct((2, own_rows,...  69 us
    squeeze x1, local copies, waits for them, and re-layouts, layer_on_device(): return (results[0], results[1])  1.53 us

profile of v7, /device:TPU:1, one launch (start us, length us, event | category | flops | bytes accessed | tf_op | source)
XLA Modules:
  0.0 71.1 jit_solution(855591831461416023)
XLA Ops:
  0.6 69.0 %shard_map.122 = bf16[2,8,4096]{2,1,0:T(8,128)(2,1)} custom-call(bf16[128,512]{1,0:T(8,128)(2,1)} %queries.1, bf16[128,512]{1,0:T(8,128)(2,1)} %keys.1, bf16[128,512]{1,0:T(8,128)(2,1)} %values.1, bf16[8,4096]{1,0:T(8,128)(2,1)} %residual.1, f32[1,4096]{1,0:T(1,128)} %bitcast.5, s32[8,8]{1,0:T(8,128)} %expert_ids.1, f32[8,8]{1,0:T(8,128)} %expert_gates.1, ...), custom_call_target="tpu_custom_call" | custom-call | flops 6979321856 | bytes 25165824 | tf_op jit(solution)/shard_map/pallas_call | solution.py:624
  69.6 1.5 %slice_bitcast_fusion = (bf16[8,4096]{1,0:T(8,128)(2,1)}, bf16[8,4096]{1,0:T(8,128)(2,1)}) fusion(bf16[2,8,4096]{2,1,0:T(8,128)(2,1)} %shard_map.122), kind=kLoop, calls=%fused_computation | loop fusion | bytes 262144 | tf_op jit(solution)/shard_map/squeeze | solution.py:649
